TPU v7x, 128 devices: a whole 4x4x4 slice. The times are simulated.
128 devices in a mesh: machine: 32 (over x, y, core), local: 4 (over z).
Axes of the slice: x: 4, y: 4, z: 4, core: 2. Of those that a mesh axis runs over, the one named last changes fastest.
Arguments:
- inputs: bfloat16 [32, 1024, 1984], P('machine', 'local'), may hold values from -6 to 6
- out_grads: bfloat16 [32, 1024, 7936], P('machine', 'local'), may hold values from -0.046875 to 0.046875
- error_buf: bfloat16 [32, 1984, 7936], P('machine', 'local'), may hold values from -4 to 4
- q_prev: bfloat16 [7936, 128], replicated, may hold values from -0.0625 to 0.0625
Outputs:
- q_factor: float32 [7936, 128], P('local')
- error_next: bfloat16 [32, 1984, 7936], P('machine', 'local')
All inputs are finite; a program needn't handle non-finite values.
Results may differ from a plain program's by a relative error of at most 0.0007.
Values may be sent and summed in bfloat16 or wider, within the bound.
A program may use at most 128 MiB of HBM per device.

v0:
```python
import jax
import jax.numpy as jnp
from jax import lax
from jax.sharding import PartitionSpec as P


def per_device(inputs, out_grads, error_buf, q_prev):
    highest = lax.Precision.HIGHEST
    row_count = error_buf.shape[1]
    first = lax.axis_index("local") * row_count
    machines = lax.axis_size("machine")
    xpart = lax.all_gather(inputs, "local", axis=1, tiled=True)
    gpart = lax.all_gather(out_grads, "local", axis=1, tiled=True)
    xrows = lax.dynamic_slice_in_dim(xpart[0], first, row_count, 1)
    grad = lax.dot_general(
        xrows, gpart[0], (((0,), (0,)), ((), ())), preferred_element_type=jnp.float32
    )
    merged = grad + error_buf[0].astype(jnp.float32)
    q_wide = q_prev.astype(jnp.float32)
    p_local = jnp.dot(merged, q_wide, precision=highest)
    p_mine = lax.psum(p_local, "machine") / machines
    gram = lax.psum(jnp.dot(p_mine.T, p_mine, precision=highest), "local")
    chol = jnp.linalg.cholesky(gram)
    p_hat = lax.linalg.triangular_solve(chol, p_mine, left_side=False, lower=True, transpose_a=True)
    q_term = lax.dot_general(merged, p_hat, (((0,), (0,)), ((), ())), precision=highest)
    q_part = lax.psum_scatter(q_term, "local", scatter_dimension=0, tiled=True)
    q_mine = lax.psum(q_part, "machine") / machines
    q_full = lax.all_gather(q_mine, "local", axis=0, tiled=True)
    update = lax.dot_general(p_hat, q_full, (((1,), (1,)), ((), ())), precision=highest)
    error_next = (merged - update).astype(jnp.bfloat16)[None]
    return (q_mine, error_next)


def solution(mesh):
    in_specs = (
        P("machine", "local", None),
        P("machine", "local", None),
        P("machine", "local", None),
        P(),
    )
    out_specs = (P("local", None), P("machine", "local", None))
    return jax.shard_map(
        per_device, mesh=mesh, in_specs=in_specs, out_specs=out_specs, check_vma=False
    )
```

profile of v0, /device:TPU:0, one launch (start us, length us, event | category | flops | bytes accessed | tf_op | source)
XLA Modules:
  0.0 676.1 jit_solution(10962967315243975583)
XLA Ops:
  7.2 0.0 copy-start
  7.2 0.0 all-gather.4.cloned.1.call-start
  7.2 0.7 all-gather.4.cloned.1.call-update
  7.9 0.0 all-gather.6.cloned.1.call-start
  8.0 0.7 all-gather.6.cloned.1.call-update
  8.7 0.0 all-reduce.4.cloned.1.call-start
  8.7 54.6 %all-gather.4.cloned.1.call-done = bf16[1,1024,1984]{1,2,0:T(8,128)(2,1)} async-done(((bf16[1,256,1984]{1,2,0:T(8,128)(2,1)}), bf16[1,1024,1984]{1,2,0:T(8,128)(2,1)}) %all-gather.4.cloned.1.call-update) | async-done | bytes 4063248 | tf_op jit(solution)/shard_map/all_gather | solution.py:12
  63.3 152.2 %all-gather.6.cloned.1.call-done = bf16[1,1024,7936]{2,1,0:T(8,128)(2,1)} async-done(((bf16[1,256,7936]{2,1,0:T(8,128)(2,1)}), bf16[1,1024,7936]{2,1,0:T(8,128)(2,1)}) %all-gather.6.cloned.1.call-update) | async-done | bytes 16252944 | tf_op jit(solution)/shard_map/all_gather | solution.py:13
  215.5 18.7 %convert_add_fusion = f32[496,7936]{1,0:T(8,128)} fusion(bf16[1,1024,7936]{2,1,0:T(8,128)(2,1)} %all-gather.6.cloned.1.call-done, bf16[1,496,7936]{2,1,0:T(8,128)(2,1)} %param.6, bf16[1,1024,1984]{1,2,0:T(8,128)(2,1)} %all-gather.4.cloned.1.call-done, s32[]{:T(128)S(6)} %select_n.7), kind=kOutput, calls=%fused_computation.2 | convolution fusion | flops 8069324800 | bytes 40886276 | tf_op jit(solution)/shard_map/dot_general | solution.py:15
  234.1 0.0 copy-done
  234.1 10.9 %fusion.19 = f32[496,128]{1,0:T(8,128)} fusion(f32[496,7936]{1,0:T(8,128)} %convert_add_fusion, bf16[7936,128]{1,0:T(8,128)(2,1)S(1)} %copy-done), kind=kOutput, calls=%fused_computation.26 | convolution fusion | flops 6046089216 | bytes 18030592 | tf_op jit(solution)/shard_map/dot_general | solution.py:20
  245.0 0.0 all-reduce.4.cloned.1.call-update
  245.0 0.0 all-reduce.6.cloned.1.call-start
  245.1 102.2 %all-reduce.4.cloned.1.call-done = f32[496,128]{1,0:T(8,128)} async-done(((f32[496,128]{1,0:T(8,128)}), f32[496,128]{1,0:T(8,128)}) %all-reduce.4.cloned.1.call-update) | async-done | bytes 253968 | tf_op jit(solution)/shard_map/psum | solution.py:21
  347.3 2.3 fusion.9
  349.6 0.0 all-reduce.6.cloned.1.call-update
  349.6 0.2 reduce-scatter.2.cloned.1.call-start
  349.9 41.1 %all-reduce.6.cloned.1.call-done = f32[128,128]{0,1:T(8,128)} async-done(((f32[128,128]{0,1:T(8,128)}), f32[128,128]{0,1:T(8,128)}) %all-reduce.6.cloned.1.call-update) | async-done | bytes 65552 | tf_op jit(solution)/shard_map/psum | solution.py:22
  390.9 0.9 copy.7
  391.9 0.9 fusion.15
  392.7 11.7 %cholesky.16 = f32[128,128]{1,0:T(8,128)S(1)} custom-call(f32[128,128]{1,0:T(8,128)S(1)} %fusion.15), custom_call_target="Cholesky" | custom-call | tf_op jit(solution)/shard_map/jit(cholesky)/cholesky | solution.py:23
  404.5 0.6 compare_reduce_fusion
  405.1 0.7 fusion.13
  405.8 9.8 %custom-call.6 = f32[1,128,128]{1,2,0:T(8,128)S(1)} custom-call(f32[1,128,128]{2,1,0:T(8,128)S(1)} %fusion.13), custom_call_target="InvertDiagBlocksLowerTriangular" | custom-call | tf_op jit(solution)/shard_map/triangular_solve | solution.py:24
  415.6 1.3 fusion.7
  416.9 30.0 %fusion.20 = f32[7936,128]{1,0:T(8,128)} fusion(f32[496,7936]{1,0:T(8,128)} %convert_add_fusion, f32[496,128]{1,0:T(8,128)S(1)} %fusion.7), kind=kOutput, calls=%fused_computation.27 | convolution fusion | flops 6046089216 | bytes 20062208 | tf_op jit(solution)/shard_map/dot_general | solution.py:25
  446.9 0.0 reduce-scatter.2.cloned.1.call-update
  446.9 0.0 all-reduce.8.cloned.1.call-start
  447.0 46.3 %reduce-scatter.2.cloned.1.call-done = f32[1984,128]{1,0:T(8,128)} async-done(((f32[7936,128]{1,0:T(8,128)}), f32[1984,128]{1,0:T(8,128)}) %reduce-scatter.2.cloned.1.call-update) | async-done | bytes 1015824 | tf_op jit(solution)/shard_map/reduce_scatter | solution.py:26
  493.3 0.0 all-reduce.8.cloned.1.call-update
  493.3 0.0 all-gather.8.cloned.1.call-start
  493.4 107.3 %all-reduce.8.cloned.1.call-done = f32[1984,128]{1,0:T(8,128)} async-done(((f32[1984,128]{1,0:T(8,128)}), f32[1984,128]{1,0:T(8,128)}) %all-reduce.8.cloned.1.call-update) | async-done | bytes 1015824 | tf_op jit(solution)/shard_map/psum | solution.py:27
  600.7 2.2 broadcast_multiply_fusion
  602.9 0.0 all-gather.8.cloned.1.call-update
  602.9 47.3 %all-gather.8.cloned.1.call-done = f32[7936,128]{1,0:T(8,128)} async-done(((f32[1984,128]{1,0:T(8,128)}), f32[7936,128]{1,0:T(8,128)}) %all-gather.8.cloned.1.call-update) | async-done | bytes 4063248 | tf_op jit(solution)/shard_map/all_gather | solution.py:28
  650.2 0.0 copy-start.1
  650.2 19.0 %fusion.4 = bf16[1,496,7936]{2,1,0:T(8,128)(2,1)} fusion(f32[496,7936]{1,0:T(8,128)} %convert_add_fusion, f32[496,128]{1,0:T(8,128)S(1)} %fusion.7, f32[7936,128]{1,0:T(8,128)} %all-gather.8.cloned.1.call-done), kind=kOutput, calls=%fused_computation.4 | convolution fusion | flops 6053961728 | bytes 27934720 | tf_op jit(solution)/shard_map/dot_general | solution.py:29
  669.2 0.0 copy-done.1
  (1 shorter events, 0.0 us)
Async XLA Ops:
  7.2 227.0 %copy-start = (bf16[7936,128]{1,0:T(8,128)(2,1)S(1)}, bf16[7936,128]{1,0:T(8,128)(2,1)}, u32[]{:S(2)}) copy-start(bf16[7936,128]{1,0:T(8,128)(2,1)} %param.7) | copy-start | bytes 6094852
  7.2 56.1 %all-gather.4.cloned.1.call-start = ((), (), s32[]{:S(2)}) async-start(), calls=%async_computation.1 | async-start | bytes 5079040 | tf_op jit(solution)/shard_map/all_gather | solution.py:12
  7.9 207.5 %all-gather.6.cloned.1.call-start = ((), (), s32[]{:S(2)}) async-start(), calls=%async_computation.2 | async-start | bytes 20316160 | tf_op jit(solution)/shard_map/all_gather | solution.py:13
  8.7 338.6 %all-reduce.4.cloned.1.call-start = ((), (), s32[]{:S(2)}) async-start(), calls=%async_computation.3 | async-start | bytes 507904 | tf_op jit(solution)/shard_map/psum | solution.py:21
  245.0 145.9 %all-reduce.6.cloned.1.call-start = ((), (), s32[]{:S(2)}) async-start(), calls=%async_computation.4 | async-start | bytes 131072 | tf_op jit(solution)/shard_map/psum | solution.py:22
  349.6 143.7 %reduce-scatter.2.cloned.1.call-start = ((), (), s32[]{:S(2)}) async-start(), calls=%async_computation.5 | async-start | bytes 5079040 | tf_op jit(solution)/shard_map/reduce_scatter | solution.py:26
  446.9 153.7 %all-reduce.8.cloned.1.call-start = ((), (), s32[]{:S(2)}) async-start(), calls=%async_computation.6 | async-start | bytes 2031616 | tf_op jit(solution)/shard_map/psum | solution.py:27
  493.3 156.9 %all-gather.8.cloned.1.call-start = ((), (), s32[]{:S(2)}) async-start(), calls=%async_computation.7 | async-start | bytes 5079040 | tf_op jit(solution)/shard_map/all_gather | solution.py:28
  650.2 19.0 %copy-start.1 = (bf16[7936,128]{1,0:T(8,128)(2,1)S(1)}, bf16[7936,128]{1,0:T(8,128)(2,1)}, u32[]{:S(2)}) copy-start(bf16[7936,128]{1,0:T(8,128)(2,1)} %param.7) | copy-start | bytes 6094852
Sparse Core Ops, SparseCore 0:
  9.7 53.5 all-gather.3
  64.9 150.4 all-gather.5
  245.2 102.1 all-reduce.3
  350.2 40.7 all-reduce.5
  447.1 46.1 reduce-scatter.1
  496.4 104.2 all-reduce.7
  603.0 47.1 all-gather.7
where the time goes:
time: 677 us; the launch traced here: 676 us
  waiting for transfers between devices  552 us (82%)
  matrix products  82.2 us (12%)
  other arithmetic  25.9 us (4%)
  between operations  14.2 us (2%)
    all_gather x1, waiting for transfers between devices, per_device(): gpart = lax.all_gather(out_grads, 'local', axis=1, tiled=True)  152 us
    psum x1, waiting for transfers between devices, per_device(): q_mine = lax.psum(q_part, 'machine') / machines  107 us
    psum x1, waiting for transfers between devices, per_device(): p_mine = lax.psum(p_local, 'machine') / machines  102 us
    all_gather x1, waiting for transfers between devices, per_device(): xpart = lax.all_gather(inputs, 'local', axis=1, tiled=True)  54.6 us
    all_gather x1, waiting for transfers between devices, per_device(): q_full = lax.all_gather(q_mine, 'local', axis=0, tiled=True)  47.3 us
    reduce_scatter x1, waiting for transfers between devices, per_device(): q_part = lax.psum_scatter(q_term, 'local', scatter_dimension=0, tiled=True)  46.3 us
    psum x1, waiting for transfers between devices, per_device(): gram = lax.psum(jnp.dot(p_mine.T, p_mine, precision=highest), 'local')  41.1 us
    dot_general x1, matrix products, per_device(): lax.dot_general(merged, p_hat, (((0,), (0,)), ((), ())), precision=highest)  30 us
  transfers between devices with their start and end apart: 7, of which 7 were waited for; matrix products, arithmetic and copies ran while one was open for 0% of the time, Pallas kernels for 0%

commit v1 on v0

v1 whole, which is shorter than its diff:
```python
import jax
import jax.numpy as jnp
from jax import lax
from jax.experimental import pallas as pl
from jax.experimental.pallas import tpu as pltpu
from jax.sharding import PartitionSpec as P

MESH = pl.DeviceIdType.MESH
F32, BF16 = jnp.float32, jnp.bfloat16
HIGHEST = lax.Precision.HIGHEST

NX, NY, NC, NZ = 4, 4, 2, 4
TOKENS, ROWS, COLS, RANK = 256, 1984, 7936, 128
MY_ROWS = ROWS // NZ
HALF = TOKENS // 2
CHUNK = 256
CHUNKS = COLS // CHUNK
P_ROWS = 2048
P_SLICE = P_ROWS // 32
PIECES = ((0, 8), (8, 16), (16, 24), (24, 31))
N_PIECE = len(PIECES)
N_COPY = 29


def dot(a, b, lhs=1, rhs=0, precision=None):
    return lax.dot_general(
        a, b, (((lhs,), (rhs,)), ((), ())), precision=precision, preferred_element_type=F32
    )


def split(value):
    high = value.astype(BF16)
    return high, (value - high.astype(F32)).astype(BF16)


def all_reduce(part, from_core, r1x, r1y, r2x, r2y, rz, full, send, recv, place, scale):
    x, y, core, z = place
    height = part.shape[3]
    upper, lower = pl.ds(0, height // 2), pl.ds(height // 2, height // 2)
    running = {}

    def start(key, number, src, dst, where):
        px, py, pcore, pz = where
        copy = pltpu.make_async_remote_copy(
            src_ref=src, dst_ref=dst, send_sem=send.at[number], recv_sem=recv.at[number],
            device_id={"machine": (px * NY + py) * NC + pcore, "local": pz}, device_id_type=MESH,
        )
        copy.start()
        running.setdefault(key, []).append(copy)

    def arrive(key):
        for copy in running[key]:
            copy.wait_recv()

    def begin():
        start("core", 0, part.at[1 - core], from_core, (x, y, 1 - core, z))

    def first():
        arrive("core")

        def add(s, carry):
            a, b = s // NY, s % NY
            part[core, a, b] = part[core, a, b] + from_core[a, b]
            return carry

        lax.fori_loop(0, NX * NY, add, 0)
        for d in range(1, 4):
            px, py = (x + d) % NX, (y + d) % NY
            start("1x", 0 + d, part.at[core, px, :, upper], r1x.at[d - 1], (px, y, core, z))
            start("1y", 3 + d, part.at[core, :, py, lower], r1y.at[d - 1], (x, py, core, z))

    def second():
        arrive("1x")
        arrive("1y")
        for b in range(NY):
            part[core, x, b, upper] = part[core, x, b, upper] + r1x[0, b] + r1x[1, b] + r1x[2, b]
        for a in range(NX):
            part[core, a, y, lower] = part[core, a, y, lower] + r1y[0, a] + r1y[1, a] + r1y[2, a]
        for d in range(1, 4):
            px, py = (x + d) % NX, (y + d) % NY
            start("2y", 6 + d, part.at[core, x, py, upper], r2y.at[d - 1], (x, py, core, z))
            start("2x", 9 + d, part.at[core, px, y, lower], r2x.at[d - 1], (px, y, core, z))

    def across():
        arrive("2x")
        arrive("2y")
        rz[z, upper] = part[core, x, y, upper] + r2y[0] + r2y[1] + r2y[2]
        rz[z, lower] = part[core, x, y, lower] + r2x[0] + r2x[1] + r2x[2]
        for d in range(1, 4):
            start("z", 12 + d, rz.at[z], rz.at[z], (x, y, core, (z + d) % NZ))

    def total():
        arrive("z")
        full[core, x, y] = (rz[0] + rz[1] + rz[2] + rz[3]) * scale
        for d in range(1, 4):
            px, py = (x + d) % NX, (y + d) % NY
            mine = full.at[core, x, y, upper]
            start("3y", 15 + d, mine, mine, (x, py, core, z))
            mine = full.at[core, x, y, lower]
            start("3x", 18 + d, mine, mine, (px, y, core, z))

    def spread():
        arrive("3x")
        arrive("3y")
        for d in range(1, 4):
            px, py = (x + d) % NX, (y + d) % NY
            mine = full.at[core, x, :, upper]
            start("4x", 21 + d, mine, mine, (px, y, core, z))
            mine = full.at[core, :, y, lower]
            start("4y", 24 + d, mine, mine, (x, py, core, z))

    def share():
        arrive("4x")
        arrive("4y")
        start("share", 28, full.at[core], full.at[core], (x, y, 1 - core, z))

    def end():
        arrive("share")

    def sent():
        for copies in running.values():
            for copy in copies:
                copy.wait_send()

    return [begin, first, second, across, total, spread, share, end], sent


def cholesky_inverse(mat):
    lane = lax.broadcasted_iota(jnp.int32, (8, RANK), 1)
    sub = lax.broadcasted_iota(jnp.int32, (8, RANK), 0)

    def panel(b, carry):
        rows = pl.ds(pl.multiple_of(b * 8, 8), 8)
        left = pltpu.roll(mat[rows, 0:RANK], (RANK - b * 8) % RANK, 1)
        right = mat[rows, RANK : 2 * RANK]
        for j in range(8):
            column = jnp.broadcast_to(left[:, j : j + 1], (8, RANK))
            pivot = jnp.broadcast_to(column[j : j + 1, :], (8, RANK))
            inv = lax.rsqrt(pivot)
            inv = inv * (1.5 - 0.5 * pivot * inv * inv)
            row_l = jnp.broadcast_to(left[j : j + 1, :], (8, RANK)) * inv
            row_r = jnp.broadcast_to(right[j : j + 1, :], (8, RANK)) * inv
            factor = column * inv
            left = jnp.where(sub > j, left - factor * row_l, jnp.where(sub == j, row_l, left))
            right = jnp.where(sub > j, right - factor * row_r, jnp.where(sub == j, row_r, right))
        left = pltpu.roll(left, b * 8, 1)
        mat[rows, 0:RANK] = left
        mat[rows, RANK : 2 * RANK] = right
        below = jnp.where(lane >= (b + 1) * 8, left, 0.0)
        both = jnp.concatenate([left, right], axis=1)
        mat[...] = mat[...] - dot(below, both, 0, 0, HIGHEST)
        return carry

    lax.fori_loop(0, RANK // 8, panel, 0)


def kernel(
    xt_hbm, g_hbm, e_hbm, q_hbm, qf_hbm, err_hbm,
    xt, xr, g_all, e_buf, q_in, p_flat, t_acc, mat, p_hat, p_mine, y_cat, p_cat, q_lines,
    p_part, p_core, p1x, p1y, p2x, p2y, p_z, p_full,
    q_part, q_core, q1x, q1y, q2x, q2y, q_z, q_full,
    load, store, p_send, p_recv, q_send, q_recv, x_send, x_recv, g_send, g_recv,
):
    m, z = lax.axis_index("machine"), lax.axis_index("local")
    core, y, x = m % NC, (m // NC) % NY, m // (NC * NY)
    place = (x, y, core, z)
    left, right = (z + NZ - 1) % NZ, (z + 1) % NZ

    loads = [
        pltpu.make_async_copy(g_hbm, g_all.at[pl.ds(z * TOKENS, TOKENS)], load.at[0]),
        pltpu.make_async_copy(q_hbm, q_in, load.at[1]),
        pltpu.make_async_copy(xt_hbm, xt.at[pl.ds(0, ROWS)], load.at[2]),
        pltpu.make_async_copy(e_hbm, e_buf, load.at[3]),
        pltpu.make_async_copy(
            xt_hbm.at[pl.ds(z * MY_ROWS, MY_ROWS)], xr.at[:, pl.ds(z * TOKENS, TOKENS)], load.at[4]
        ),
    ]
    for copy in loads:
        copy.start()

    with jax.named_scope("barrier"):
        barrier = pltpu.get_barrier_semaphore()
        for d in range(1, 4):
            for px, py, pcore, pz in (
                ((x + d) % NX, y, core, z), (x, (y + d) % NY, core, z), (x, y, core, (z + d) % NZ)
            ):
                pl.semaphore_signal(
                    barrier, inc=1, device_id_type=MESH,
                    device_id={"machine": (px * NY + py) * NC + pcore, "local": pz},
                )
        pl.semaphore_signal(
            barrier, inc=1, device_id_type=MESH,
            device_id={"machine": (x * NY + y) * NC + 1 - core, "local": z},
        )
        pl.semaphore_wait(barrier, 10)

    x_copies = []
    for d in range(1, 4):
        pz = (z + d) % NZ
        x_copies.append(pltpu.make_async_remote_copy(
            src_ref=xt_hbm.at[pl.ds(pz * MY_ROWS, MY_ROWS)],
            dst_ref=xr.at[:, pl.ds(z * TOKENS, TOKENS)],
            send_sem=x_send.at[d], recv_sem=x_recv.at[d],
            device_id={"machine": m, "local": pz}, device_id_type=MESH,
        ))
        x_copies[-1].start()

    def g_copy(src, dst, kind, piece, half, owner, target):
        first, last = PIECES[piece]
        rows = pl.ds(owner * TOKENS + half * HALF, HALF)
        cols = pl.ds(first * CHUNK, (last - first) * CHUNK)
        dst = dst.at[rows, cols]
        src = dst if src is None else src.at[pl.ds(half * HALF, HALF), cols]
        return pltpu.make_async_remote_copy(
            src_ref=src, dst_ref=dst, send_sem=g_send.at[kind, piece], recv_sem=g_recv.at[kind, piece],
            device_id={"machine": m, "local": target}, device_id_type=MESH,
        )

    early, late, onward = [], [], []
    for i in range(N_PIECE):
        early += [g_copy(g_hbm, g_all, 0, i, 0, z, right), g_copy(g_hbm, g_all, 1, i, 1, z, left)]
        late += [g_copy(g_hbm, g_all, 2, i, 1, z, right), g_copy(g_hbm, g_all, 3, i, 0, z, left)]
        onward += [g_copy(None, g_all, 4, i, 0, left, right), g_copy(None, g_all, 5, i, 1, right, left)]
    for copy in early:
        copy.start()

    p_steps, p_sent = all_reduce(
        p_part, p_core, p1x, p1y, p2x, p2y, p_z, p_full, p_send, p_recv, place, 1.0 / 32
    )
    q_steps, q_sent = all_reduce(
        q_part, q_core, q1x, q1y, q2x, q2y, q_z, q_full, q_send, q_recv, place, 1.0 / 32
    )

    with jax.named_scope("left_terms"):
        xt[pl.ds(ROWS, P_ROWS - ROWS)] = jnp.zeros((P_ROWS - ROWS, TOKENS), BF16)
        loads[1].wait()
        loads[0].wait()
        t_acc[...] = jnp.zeros_like(t_acc)

        def token_terms(s, carry):
            cols = pl.ds(pl.multiple_of(s * CHUNK, CHUNK), CHUNK)
            t_acc[...] += dot(g_all[pl.ds(pl.multiple_of(z * TOKENS, TOKENS), TOKENS), cols], q_in[cols, :])
            return carry

        lax.fori_loop(0, CHUNKS, token_terms, 0)
        t_high, t_low = split(t_acc[...])
        loads[2].wait()
        p_flat[...] = dot(xt[...], t_high) + dot(xt[...], t_low)
        loads[3].wait()
        mine = pl.ds(pl.multiple_of(z * MY_ROWS, 8), MY_ROWS)

        def error_terms(s, carry):
            cols = pl.ds(pl.multiple_of(s * CHUNK, CHUNK), CHUNK)
            p_flat[mine, :] += dot(e_buf[:, cols], q_in[cols, :])
            return carry

        lax.fori_loop(0, CHUNKS, error_terms, 0)
        p_part[...] = p_flat[...].reshape(p_part.shape)

    with jax.named_scope("left_reduce"):
        for step in p_steps:
            step()

    for copy in late:
        copy.start()

    with jax.named_scope("factor"):
        p_flat[...] = p_full[...].reshape(P_ROWS, RANK)
        mat[:, 0:RANK] = dot(p_flat[...], p_flat[...], 0, 0, HIGHEST)
        diagonal = lax.broadcasted_iota(jnp.int32, (RANK, RANK), 0) == lax.broadcasted_iota(
            jnp.int32, (RANK, RANK), 1
        )
        mat[:, RANK : 2 * RANK] = jnp.where(diagonal, 1.0, 0.0)
    with jax.named_scope("cholesky"):
        cholesky_inverse(mat)

    with jax.named_scope("right_terms"):
        p_hat[...] = dot(p_flat[...], mat[:, RANK : 2 * RANK], 1, 1, HIGHEST)
        high, low = split(p_hat[...])
        y_high, y_low = split(dot(high, xt[...], 0, 0) + dot(low, xt[...], 0, 0))
        y_cat[0:RANK, :] = y_high
        y_cat[RANK : 2 * RANK, :] = y_low
        p_mine[...] = p_hat[mine, :]
        m_high, m_low = split(p_mine[...])
        p_cat[:, 0:RANK] = m_high
        p_cat[:, RANK : 2 * RANK] = m_low
        p_cat[:, 2 * RANK : 3 * RANK] = m_high

        def right_terms(s, carry):
            cols = pl.ds(pl.multiple_of(s * CHUNK, CHUNK), CHUNK)
            g_rows = pl.ds(pl.multiple_of(z * TOKENS, TOKENS), TOKENS)
            both = dot(y_cat[...], g_all[g_rows, cols]) + dot(p_cat[:, 0 : 2 * RANK], e_buf[:, cols], 0, 0)
            q_part[s // 16, (s // 4) % 4, s % 4] = both[0:RANK] + both[RANK : 2 * RANK]
            return carry

        lax.fori_loop(0, CHUNKS, right_terms, 0)
        q_part[1, 3, 3] = jnp.zeros((RANK, CHUNK), F32)

    with jax.named_scope("pass_on"):
        for own, passed in zip(early, onward):
            own.wait_recv()
            passed.start()

    for name, step in zip(
        ("q_begin", "q_first", "q_second", "q_across", "q_total", "q_spread", "q_share", "q_end"), q_steps
    ):
        with jax.named_scope(name):
            step()

    with jax.named_scope("right_factor"):
        first_line = (31 * z) // 4

        def lines(i, carry):
            s = first_line + i
            q_lines[pl.ds(pl.multiple_of(i * CHUNK, CHUNK), CHUNK), :] = q_full[
                s // 16, (s // 4) % 4, s % 4
            ].T
            return carry

        lax.fori_loop(0, 9, lines, 0)
        offset = (CHUNK - 64 * z) % CHUNK
        qf_store = pltpu.make_async_copy(q_lines.at[pl.ds(offset, ROWS)], qf_hbm, store.at[0])
        qf_store.start()

    loads[4].wait()
    for copy in x_copies:
        copy.wait_recv()
    stores = [qf_store]
    for i in range(N_PIECE):
        first, last = PIECES[i]
        with jax.named_scope("error_wait"):
            for copy in late[2 * i : 2 * i + 2] + onward[2 * i : 2 * i + 2]:
                copy.wait_recv()

        def error_chunk(s, carry):
            cols = pl.ds(pl.multiple_of(s * CHUNK, CHUNK), CHUNK)
            q_high, q_low = split(q_full[s // 16, (s // 4) % 4, s % 4])
            merged = dot(xr[...], g_all[:, cols]) + e_buf[:, cols].astype(F32)
            update = dot(p_cat[...], jnp.concatenate([q_high, q_high, q_low], axis=0))
            e_buf[:, cols] = (merged - update).astype(BF16)
            return carry

        with jax.named_scope("error_next"):
            lax.fori_loop(first, last, error_chunk, 0)
        cols = pl.ds(first * CHUNK, (last - first) * CHUNK)
        stores.append(pltpu.make_async_copy(e_buf.at[:, cols], err_hbm.at[:, cols], store.at[1 + i]))
        stores[-1].start()

    with jax.named_scope("finish"):
        p_sent()
        q_sent()
        for copy in x_copies + early + late + onward:
            copy.wait_send()
        for copy in stores:
            copy.wait()


def per_device(inputs, out_grads, error_buf, q_prev):
    any_space = pl.BlockSpec(memory_space=pl.ANY)

    def reduce_scratch(height, width):
        stage = pltpu.VMEM((3, 4, height // 2, width), F32)
        small = pltpu.VMEM((3, height // 2, width), F32)
        return [
            pltpu.VMEM((NC, NX, NY, height, width), F32),
            pltpu.VMEM((NX, NY, height, width), F32),
            stage, stage, small, small,
            pltpu.VMEM((NZ, height, width), F32),
            pltpu.VMEM((NC, NX, NY, height, width), F32),
        ]

    dma = pltpu.SemaphoreType.DMA
    q_factor, error_next = pl.pallas_call(
        kernel,
        out_shape=(
            jax.ShapeDtypeStruct((ROWS, RANK), F32),
            jax.ShapeDtypeStruct((MY_ROWS, COLS), BF16),
        ),
        in_specs=[any_space] * 4,
        out_specs=(any_space, any_space),
        scratch_shapes=[
            pltpu.VMEM((P_ROWS, TOKENS), BF16),
            pltpu.VMEM((MY_ROWS, NZ * TOKENS), BF16),
            pltpu.VMEM((NZ * TOKENS, COLS), BF16),
            pltpu.VMEM((MY_ROWS, COLS), BF16),
            pltpu.VMEM((COLS, RANK), BF16),
            pltpu.VMEM((P_ROWS, RANK), F32),
            pltpu.VMEM((TOKENS, RANK), F32),
            pltpu.VMEM((RANK, 2 * RANK), F32),
            pltpu.VMEM((P_ROWS, RANK), F32),
            pltpu.VMEM((MY_ROWS, RANK), F32),
            pltpu.VMEM((2 * RANK, TOKENS), BF16),
            pltpu.VMEM((MY_ROWS, 3 * RANK), BF16),
            pltpu.VMEM((9 * CHUNK, RANK), F32),
            *reduce_scratch(P_SLICE, RANK),
            *reduce_scratch(RANK, CHUNK),
            dma((5,)), dma((1 + N_PIECE,)),
            dma((N_COPY,)), dma((N_COPY,)), dma((N_COPY,)), dma((N_COPY,)),
            dma((4,)), dma((4,)), dma((6, N_PIECE)), dma((6, N_PIECE)),
        ],
        compiler_params=pltpu.CompilerParams(
            collective_id=0, has_side_effects=True, vmem_limit_bytes=60 * 1024 * 1024
        ),
    )(inputs[0].T, out_grads[0], error_buf[0], q_prev)
    return q_factor, error_next[None]


def solution(mesh):
    in_specs = (
        P("machine", "local", None),
        P("machine", "local", None),
        P("machine", "local", None),
        P(),
    )
    out_specs = (P("local", None), P("machine", "local", None))
    return jax.shard_map(
        per_device, mesh=mesh, in_specs=in_specs, out_specs=out_specs, check_vma=False
    )
```

time: 677 us -> 225 us (0.33)
  waiting for transfers between devices: 552 us -> 0 us
  Pallas kernels: 0 us -> 213 us
  matrix products: 82.2 us -> 0 us
  other arithmetic: 25.9 us -> 0 us
  between operations: 14.2 us -> 0.64 us
  local copies, waits for them, and re-layouts: 0.94 us -> 9.2 us
    all_gather x3 -> x0, waiting for transfers between devices: 254 us -> none  [the longest x1 152 us: per_device(): gpart = lax.all_gather(out_grads, 'local', axis=1, tiled=True)]
    psum x3 -> x0, waiting for transfers between devices: 251 us -> none  [the longest x1 107 us: per_device(): q_mine = lax.psum(q_part, 'machine') / machines]
    pallas_call x0 -> x1, Pallas kernels: none -> 213 us  [per_device(): pl.pallas_call(kernel, out_shape=(jax.ShapeDtypeStruct((ROWS, RANK), F32)...]
    dot_general x5 -> x0, matrix products: 80.9 us -> none  [the longest x1 30 us: per_device(): lax.dot_general(merged, p_hat, (((0,), (0,)), ((), ())), precision=highest)]
    reduce_scatter x1 -> x0, waiting for transfers between devices: 46.3 us -> none  [per_device(): q_part = lax.psum_scatter(q_term, 'local', scatter_dimension=0, tiled=True)]
    another operation x5 -> x0, other arithmetic: 22.9 us -> none  [the longest x3 12.4 us: per_device(): chol = jnp.linalg.cholesky(gram)]
    unnamed x4 -> x2, local copies, waits for them, and re-layouts: 0.02 us -> 9.2 us
  transfers between devices with their start and end apart: 7 -> 0, of which waited for: 7 -> 0; matrix products, arithmetic and copies ran while one was open for 0% -> 0% of each run, Pallas kernels for 0% -> 0%
where the time goes in v1:
time: 225 us; the launch traced here: 223 us
  Pallas kernels  213 us (95%)
  local copies, waits for them, and re-layouts  9.2 us (4%)
    pallas_call x1, Pallas kernels, per_device(): pl.pallas_call(kernel, out_shape=(jax.ShapeDtypeStruct((ROWS, RANK), F32)...  213 us
    unnamed x2, local copies, waits for them, and re-layouts  9.2 us

profile of v1, /device:TPU:0, one launch (start us, length us, event | category | flops | bytes accessed | tf_op | source)
XLA Modules:
  0.0 223.1 jit_solution(7090303417804652847)
XLA Ops:
  0.6 213.3 %shard_map.59 = (f32[1984,128]{1,0:T(8,128)}, bf16[496,7936]{1,0:T(8,128)(2,1)}) custom-call(bf16[1984,256]{1,0:T(8,128)(2,1)} %bitcast.9, bf16[256,7936]{1,0:T(8,128)(2,1)} %bitcast.8, bf16[496,7936]{1,0:T(8,128)(2,1)} %bitcast.6, bf16[7936,128]{1,0:T(8,128)(2,1)} %q_hbm.1), custom_call_target="tpu_custom_call" | custom-call | tf_op jit(solution)/shard_map/pallas_call | solution.py:373
  213.9 2.2 %copy.8 = f32[1984,128]{1,0:T(8,128)} copy(f32[1984,128]{1,0:T(8,128)} %get-tuple-element.8) | data formatting | bytes 2031616
  216.2 7.0 %copy.9 = bf16[1,496,7936]{2,1,0:T(8,128)(2,1)} copy(bf16[1,496,7936]{2,1,0:T(8,128)(2,1)} %bitcast.7) | data formatting | bytes 15745024

commit v2 on v1

--- a/solution.py
+++ b/solution.py
@@ -17,9 +17,15 @@
 CHUNKS = COLS // CHUNK
 P_ROWS = 2048
 P_SLICE = P_ROWS // 32
-PIECES = ((0, 8), (8, 16), (16, 24), (24, 31))
+PIECES = ((0, 4), (4, 8), (8, 12), (12, 16), (16, 20), (20, 24), (24, 28), (28, 31))
 N_PIECE = len(PIECES)
 N_COPY = 29
+PANEL = 32
+PLAN = {
+    "start": (("x", 0, 3), ("early", 0, 2)),
+    "p4": (("early", 2, 8), ("late", 0, 4)),
+    "q4": (("late", 4, 8), ("onward", 0, 8)),
+}
 
 
 def dot(a, b, lhs=1, rhs=0, precision=None):
@@ -126,37 +132,43 @@
 
 
 def cholesky_inverse(mat):
-    lane = lax.broadcasted_iota(jnp.int32, (8, RANK), 1)
-    sub = lax.broadcasted_iota(jnp.int32, (8, RANK), 0)
+    shape = (PANEL, RANK)
+    lane = lax.broadcasted_iota(jnp.int32, shape, 1)
+    sub = lax.broadcasted_iota(jnp.int32, shape, 0)
 
     def panel(b, carry):
-        rows = pl.ds(pl.multiple_of(b * 8, 8), 8)
-        left = pltpu.roll(mat[rows, 0:RANK], (RANK - b * 8) % RANK, 1)
+        rows = pl.ds(pl.multiple_of(b * PANEL, PANEL), PANEL)
+        left = pltpu.roll(mat[rows, 0:RANK], (RANK - b * PANEL) % RANK, 1)
         right = mat[rows, RANK : 2 * RANK]
-        for j in range(8):
-            column = jnp.broadcast_to(left[:, j : j + 1], (8, RANK))
-            pivot = jnp.broadcast_to(column[j : j + 1, :], (8, RANK))
-            inv = lax.rsqrt(pivot)
-            inv = inv * (1.5 - 0.5 * pivot * inv * inv)
-            row_l = jnp.broadcast_to(left[j : j + 1, :], (8, RANK)) * inv
-            row_r = jnp.broadcast_to(right[j : j + 1, :], (8, RANK)) * inv
-            factor = column * inv
-            left = jnp.where(sub > j, left - factor * row_l, jnp.where(sub == j, row_l, left))
-            right = jnp.where(sub > j, right - factor * row_r, jnp.where(sub == j, row_r, right))
-        left = pltpu.roll(left, b * 8, 1)
+        pivots = jnp.ones(shape, F32)
+        for first in range(0, PANEL, 8):
+            columns = [jnp.broadcast_to(left[:, first + k : first + k + 1], shape) for k in range(8)]
+            for k in range(8):
+                j = first + k
+                pivot = jnp.broadcast_to(columns[k][j : j + 1, :], shape)
+                factor = jnp.where(sub > j, columns[k] * (1.0 / pivot), 0.0)
+                for n in range(k + 1, 8):
+                    columns[n] = columns[n] - factor * columns[n][j : j + 1, :]
+                left = left - factor * left[j : j + 1, :]
+                right = right - factor * right[j : j + 1, :]
+                pivots = jnp.where(sub == j, pivot, pivots)
+        scale = lax.rsqrt(pivots)
+        scale = scale * (1.5 - 0.5 * pivots * scale * scale)
+        left = pltpu.roll(left * scale, b * PANEL, 1)
+        right = right * scale
         mat[rows, 0:RANK] = left
         mat[rows, RANK : 2 * RANK] = right
-        below = jnp.where(lane >= (b + 1) * 8, left, 0.0)
+        below = jnp.where(lane >= (b + 1) * PANEL, left, 0.0)
         both = jnp.concatenate([left, right], axis=1)
         mat[...] = mat[...] - dot(below, both, 0, 0, HIGHEST)
         return carry
 
-    lax.fori_loop(0, RANK // 8, panel, 0)
+    lax.fori_loop(0, RANK // PANEL, panel, 0)
 
 
 def kernel(
-    xt_hbm, g_hbm, e_hbm, q_hbm, qf_hbm, err_hbm,
-    xt, xr, g_all, e_buf, q_in, p_flat, t_acc, mat, p_hat, p_mine, y_cat, p_cat, q_lines,
+    xt_hbm, g_hbm, e_hbm, q_hbm, qf_out, e_buf,
+    xt, xr, g_all, q_in, p_flat, t_cat, mat, p_rows, p_t, y_cat, p_cat, q_lines,
     p_part, p_core, p1x, p1y, p2x, p2y, p_z, p_full,
     q_part, q_core, q1x, q1y, q2x, q2y, q_z, q_full,
     load, store, p_send, p_recv, q_send, q_recv, x_send, x_recv, g_send, g_recv,
@@ -203,7 +215,6 @@
             send_sem=x_send.at[d], recv_sem=x_recv.at[d],
             device_id={"machine": m, "local": pz}, device_id_type=MESH,
         ))
-        x_copies[-1].start()
 
     def g_copy(src, dst, kind, piece, half, owner, target):
         first, last = PIECES[piece]
@@ -221,8 +232,21 @@
         early += [g_copy(g_hbm, g_all, 0, i, 0, z, right), g_copy(g_hbm, g_all, 1, i, 1, z, left)]
         late += [g_copy(g_hbm, g_all, 2, i, 1, z, right), g_copy(g_hbm, g_all, 3, i, 0, z, left)]
         onward += [g_copy(None, g_all, 4, i, 0, left, right), g_copy(None, g_all, 5, i, 1, right, left)]
-    for copy in early:
-        copy.start()
+    def due(point):
+        for name, first, last in PLAN.get(point, ()):
+            for i in range(first, last):
+                if name == "x":
+                    x_copies[i].start()
+                for k in (2 * i, 2 * i + 1):
+                    if name == "early":
+                        early[k].start()
+                    if name == "late":
+                        late[k].start()
+                    if name == "onward":
+                        early[k].wait_recv()
+                        onward[k].start()
+
+    due("start")
 
     p_steps, p_sent = all_reduce(
         p_part, p_core, p1x, p1y, p2x, p2y, p_z, p_full, p_send, p_recv, place, 1.0 / 32
@@ -235,34 +259,29 @@
         xt[pl.ds(ROWS, P_ROWS - ROWS)] = jnp.zeros((P_ROWS - ROWS, TOKENS), BF16)
         loads[1].wait()
         loads[0].wait()
-        t_acc[...] = jnp.zeros_like(t_acc)
-
-        def token_terms(s, carry):
-            cols = pl.ds(pl.multiple_of(s * CHUNK, CHUNK), CHUNK)
-            t_acc[...] += dot(g_all[pl.ds(pl.multiple_of(z * TOKENS, TOKENS), TOKENS), cols], q_in[cols, :])
-            return carry
-
-        lax.fori_loop(0, CHUNKS, token_terms, 0)
-        t_high, t_low = split(t_acc[...])
+        own = pl.ds(pl.multiple_of(z * TOKENS, TOKENS), TOKENS)
+        mine = pl.ds(pl.multiple_of(z * MY_ROWS, 8), MY_ROWS)
+        t_cat[...] = jnp.concatenate(
+            split(
+                dot(g_all[own, 0 : COLS // 2], q_in[0 : COLS // 2, :])
+                + dot(g_all[own, COLS // 2 : COLS], q_in[COLS // 2 : COLS, :])
+            ),
+            axis=1,
+        )
         loads[2].wait()
-        p_flat[...] = dot(xt[...], t_high) + dot(xt[...], t_low)
+        both = dot(xt[...], t_cat[...])
+        p_flat[...] = both[:, 0:RANK] + both[:, RANK : 2 * RANK]
         loads[3].wait()
-        mine = pl.ds(pl.multiple_of(z * MY_ROWS, 8), MY_ROWS)
-
-        def error_terms(s, carry):
-            cols = pl.ds(pl.multiple_of(s * CHUNK, CHUNK), CHUNK)
-            p_flat[mine, :] += dot(e_buf[:, cols], q_in[cols, :])
-            return carry
-
-        lax.fori_loop(0, CHUNKS, error_terms, 0)
+        p_flat[mine, :] += dot(e_buf[:, 0 : COLS // 2], q_in[0 : COLS // 2, :]) + dot(
+            e_buf[:, COLS // 2 : COLS], q_in[COLS // 2 : COLS, :]
+        )
         p_part[...] = p_flat[...].reshape(p_part.shape)
 
     with jax.named_scope("left_reduce"):
-        for step in p_steps:
+        for k, step in enumerate(p_steps):
+            due("p%d" % k)
             step()
-
-    for copy in late:
-        copy.start()
+    due("p8")
 
     with jax.named_scope("factor"):
         p_flat[...] = p_full[...].reshape(P_ROWS, RANK)
@@ -273,39 +292,38 @@
         mat[:, RANK : 2 * RANK] = jnp.where(diagonal, 1.0, 0.0)
     with jax.named_scope("cholesky"):
         cholesky_inverse(mat)
+    due("chol")
 
     with jax.named_scope("right_terms"):
-        p_hat[...] = dot(p_flat[...], mat[:, RANK : 2 * RANK], 1, 1, HIGHEST)
-        high, low = split(p_hat[...])
-        y_high, y_low = split(dot(high, xt[...], 0, 0) + dot(low, xt[...], 0, 0))
-        y_cat[0:RANK, :] = y_high
-        y_cat[RANK : 2 * RANK, :] = y_low
-        p_mine[...] = p_hat[mine, :]
-        m_high, m_low = split(p_mine[...])
+        inverse = mat[:, RANK : 2 * RANK]
+        p_rows[0:RANK, :], p_rows[RANK : 2 * RANK, :] = split(dot(inverse, p_flat[...], 1, 1, HIGHEST))
+        y_sum = dot(p_rows[...], xt[...])
+        y_cat[0:RANK, :], y_cat[RANK : 2 * RANK, :] = split(y_sum[0:RANK] + y_sum[RANK : 2 * RANK])
+        p_mine = p_flat[mine, :]
+        p_t[0:RANK, :], p_t[RANK : 2 * RANK, :] = split(dot(inverse, p_mine, 1, 1, HIGHEST))
+        m_high, m_low = split(dot(p_mine, inverse, 1, 1, HIGHEST))
         p_cat[:, 0:RANK] = m_high
         p_cat[:, RANK : 2 * RANK] = m_low
         p_cat[:, 2 * RANK : 3 * RANK] = m_high
 
+        q_part[1, 3, 3] = jnp.zeros((RANK, CHUNK), F32)
+
         def right_terms(s, carry):
             cols = pl.ds(pl.multiple_of(s * CHUNK, CHUNK), CHUNK)
-            g_rows = pl.ds(pl.multiple_of(z * TOKENS, TOKENS), TOKENS)
-            both = dot(y_cat[...], g_all[g_rows, cols]) + dot(p_cat[:, 0 : 2 * RANK], e_buf[:, cols], 0, 0)
+            both = dot(y_cat[...], g_all[own, cols]) + dot(p_t[...], e_buf[:, cols])
             q_part[s // 16, (s // 4) % 4, s % 4] = both[0:RANK] + both[RANK : 2 * RANK]
             return carry
 
-        lax.fori_loop(0, CHUNKS, right_terms, 0)
-        q_part[1, 3, 3] = jnp.zeros((RANK, CHUNK), F32)
-
-    with jax.named_scope("pass_on"):
-        for own, passed in zip(early, onward):
-            own.wait_recv()
-            passed.start()
-
-    for name, step in zip(
-        ("q_begin", "q_first", "q_second", "q_across", "q_total", "q_spread", "q_share", "q_end"), q_steps
-    ):
-        with jax.named_scope(name):
-            step()
+        other = (1 - core) * 16
+        lax.fori_loop(other, other + 15 + core, right_terms, 0)
+        due("q0")
+        q_steps[0]()
+        lax.fori_loop(core * 16, core * 16 + 16 - core, right_terms, 0)
+
+    for k, step in enumerate(q_steps[1:], 1):
+        due("q%d" % k)
+        step()
+    due("q8")
 
     with jax.named_scope("right_factor"):
         first_line = (31 * z) // 4
@@ -319,7 +337,7 @@
 
         lax.fori_loop(0, 9, lines, 0)
         offset = (CHUNK - 64 * z) % CHUNK
-        qf_store = pltpu.make_async_copy(q_lines.at[pl.ds(offset, ROWS)], qf_hbm, store.at[0])
+        qf_store = pltpu.make_async_copy(q_lines.at[pl.ds(offset, ROWS)], qf_out, store.at[0])
         qf_store.start()
 
     loads[4].wait()
@@ -342,9 +360,6 @@
 
         with jax.named_scope("error_next"):
             lax.fori_loop(first, last, error_chunk, 0)
-        cols = pl.ds(first * CHUNK, (last - first) * CHUNK)
-        stores.append(pltpu.make_async_copy(e_buf.at[:, cols], err_hbm.at[:, cols], store.at[1 + i]))
-        stores[-1].start()
 
     with jax.named_scope("finish"):
         p_sent()
@@ -373,33 +388,32 @@
     q_factor, error_next = pl.pallas_call(
         kernel,
         out_shape=(
-            jax.ShapeDtypeStruct((ROWS, RANK), F32),
-            jax.ShapeDtypeStruct((MY_ROWS, COLS), BF16),
+            pltpu.VMEM((ROWS, RANK), F32),
+            pltpu.VMEM((MY_ROWS, COLS), BF16),
         ),
         in_specs=[any_space] * 4,
-        out_specs=(any_space, any_space),
+        out_specs=(pl.BlockSpec(memory_space=pltpu.VMEM),) * 2,
         scratch_shapes=[
             pltpu.VMEM((P_ROWS, TOKENS), BF16),
             pltpu.VMEM((MY_ROWS, NZ * TOKENS), BF16),
             pltpu.VMEM((NZ * TOKENS, COLS), BF16),
-            pltpu.VMEM((MY_ROWS, COLS), BF16),
             pltpu.VMEM((COLS, RANK), BF16),
             pltpu.VMEM((P_ROWS, RANK), F32),
-            pltpu.VMEM((TOKENS, RANK), F32),
+            pltpu.VMEM((TOKENS, 2 * RANK), BF16),
             pltpu.VMEM((RANK, 2 * RANK), F32),
-            pltpu.VMEM((P_ROWS, RANK), F32),
-            pltpu.VMEM((MY_ROWS, RANK), F32),
+            pltpu.VMEM((2 * RANK, P_ROWS), BF16),
+            pltpu.VMEM((2 * RANK, MY_ROWS), BF16),
             pltpu.VMEM((2 * RANK, TOKENS), BF16),
             pltpu.VMEM((MY_ROWS, 3 * RANK), BF16),
             pltpu.VMEM((9 * CHUNK, RANK), F32),
             *reduce_scratch(P_SLICE, RANK),
             *reduce_scratch(RANK, CHUNK),
-            dma((5,)), dma((1 + N_PIECE,)),
+            dma((5,)), dma((1,)),
             dma((N_COPY,)), dma((N_COPY,)), dma((N_COPY,)), dma((N_COPY,)),
             dma((4,)), dma((4,)), dma((6, N_PIECE)), dma((6, N_PIECE)),
         ],
         compiler_params=pltpu.CompilerParams(
-            collective_id=0, has_side_effects=True, vmem_limit_bytes=60 * 1024 * 1024
+            collective_id=0, has_side_effects=True, vmem_limit_bytes=48 * 1024 * 1024
         ),
     )(inputs[0].T, out_grads[0], error_buf[0], q_prev)
     return q_factor, error_next[None]

time: 225 us -> 165 us (0.73)
  Pallas kernels: 213 us -> 161 us
  local copies, waits for them, and re-layouts: 9.2 us -> 4.18 us
    pallas_call x1, Pallas kernels: 213 us -> 161 us  [per_device(): pl.pallas_call(kernel, out_shape=(pltpu.VMEM((ROWS, RANK), F32), pltpu.VM...]
    unnamed x2, local copies, waits for them, and re-layouts: 9.2 us -> 4.18 us
where the time goes in v2:
time: 165 us
  Pallas kernels  161 us (98%)
  local copies, waits for them, and re-layouts  4.18 us (3%)
    pallas_call x1, Pallas kernels, per_device(): pl.pallas_call(kernel, out_shape=(pltpu.VMEM((ROWS, RANK), F32), pltpu.VM...  161 us
    unnamed x2, local copies, waits for them, and re-layouts  4.18 us

profile of v2, /device:TPU:0, one launch (start us, length us, event | category | flops | bytes accessed | tf_op | source)
XLA Modules:
  0.0 165.3 jit_solution(6806900815367498552)
XLA Ops:
  0.6 160.5 %shard_map.59 = (f32[1984,128]{1,0:T(8,128)S(1)}, bf16[496,7936]{1,0:T(8,128)(2,1)S(1)}) custom-call(bf16[1984,256]{1,0:T(8,128)(2,1)} %bitcast.9, bf16[256,7936]{1,0:T(8,128)(2,1)} %bitcast.8, bf16[496,7936]{1,0:T(8,128)(2,1)} %bitcast.7, bf16[7936,128]{1,0:T(8,128)(2,1)} %q_hbm.1), custom_call_target="tpu_custom_call" | custom-call | tf_op jit(solution)/shard_map/pallas_call | solution.py:388
  161.2 1.0 copy.8
  162.1 3.2 %copy.9 = bf16[1,496,7936]{2,1,0:T(8,128)(2,1)} copy(bf16[1,496,7936]{2,1,0:T(8,128)(2,1)S(1)} %bitcast.6) | data formatting | bytes 15745024

commit v3 on v2

--- a/solution.py
+++ b/solution.py
@@ -17,14 +17,16 @@
 CHUNKS = COLS // CHUNK
 P_ROWS = 2048
 P_SLICE = P_ROWS // 32
-PIECES = ((0, 4), (4, 8), (8, 12), (12, 16), (16, 20), (20, 24), (24, 28), (28, 31))
+PIECES = ((0, 5), (5, 10), (10, 15), (15, 20), (20, 24), (24, 28), (28, 30), (30, 31))
 N_PIECE = len(PIECES)
-N_COPY = 29
+N_COPY = 32
 PANEL = 32
 PLAN = {
     "start": (("x", 0, 3), ("early", 0, 2)),
-    "p4": (("early", 2, 8), ("late", 0, 4)),
-    "q4": (("late", 4, 8), ("onward", 0, 8)),
+    "p4": (("early", 6, 8),),
+    "p5": (("early", 2, 6), ("late", 0, 4)),
+    "q4": (("late", 6, 8),),
+    "q5": (("late", 4, 6), ("onward", 0, 8)),
 }
 
 
@@ -44,6 +46,9 @@
     height = part.shape[3]
     upper, lower = pl.ds(0, height // 2), pl.ds(height // 2, height // 2)
     running = {}
+
+    def quarter(k):
+        return pl.ds(pl.multiple_of(k * (height // NZ), 8), height // NZ)
 
     def start(key, number, src, dst, where):
         px, py, pcore, pz = where
@@ -90,14 +95,22 @@
     def across():
         arrive("2x")
         arrive("2y")
-        rz[z, upper] = part[core, x, y, upper] + r2y[0] + r2y[1] + r2y[2]
-        rz[z, lower] = part[core, x, y, lower] + r2x[0] + r2x[1] + r2x[2]
-        for d in range(1, 4):
-            start("z", 12 + d, rz.at[z], rz.at[z], (x, y, core, (z + d) % NZ))
+        part[core, x, y, upper] = part[core, x, y, upper] + r2y[0] + r2y[1] + r2y[2]
+        part[core, x, y, lower] = part[core, x, y, lower] + r2x[0] + r2x[1] + r2x[2]
+        for d in range(1, 4):
+            to = (z + d) % NZ
+            start("z", 12 + d, part.at[core, x, y, quarter(to)], rz.at[d - 1], (x, y, core, to))
 
     def total():
         arrive("z")
-        full[core, x, y] = (rz[0] + rz[1] + rz[2] + rz[3]) * scale
+        mine = quarter(z)
+        full[core, x, y, mine] = (part[core, x, y, mine] + rz[0] + rz[1] + rz[2]) * scale
+        for d in range(1, 4):
+            mine = full.at[core, x, y, quarter(z)]
+            start("zz", 28 + d, mine, mine, (x, y, core, (z + d) % NZ))
+
+    def joined():
+        arrive("zz")
         for d in range(1, 4):
             px, py = (x + d) % NX, (y + d) % NY
             mine = full.at[core, x, y, upper]
@@ -128,7 +141,7 @@
             for copy in copies:
                 copy.wait_send()
 
-    return [begin, first, second, across, total, spread, share, end], sent
+    return [begin, first, second, across, total, joined, spread, share, end], sent
 
 
 def cholesky_inverse(mat):
@@ -281,7 +294,6 @@
         for k, step in enumerate(p_steps):
             due("p%d" % k)
             step()
-    due("p8")
 
     with jax.named_scope("factor"):
         p_flat[...] = p_full[...].reshape(P_ROWS, RANK)
@@ -292,7 +304,6 @@
         mat[:, RANK : 2 * RANK] = jnp.where(diagonal, 1.0, 0.0)
     with jax.named_scope("cholesky"):
         cholesky_inverse(mat)
-    due("chol")
 
     with jax.named_scope("right_terms"):
         inverse = mat[:, RANK : 2 * RANK]
@@ -323,7 +334,6 @@
     for k, step in enumerate(q_steps[1:], 1):
         due("q%d" % k)
         step()
-    due("q8")
 
     with jax.named_scope("right_factor"):
         first_line = (31 * z) // 4
@@ -370,6 +380,17 @@
             copy.wait()
 
 
+def closing(qf_in, err_in, qf_out, err_out, done):
+    copies = [pltpu.make_async_copy(qf_in, qf_out, done.at[0])]
+    for k, (first, last) in enumerate(((0, 128), (128, 256), (256, 384), (384, MY_ROWS))):
+        rows = pl.ds(first, last - first)
+        copies.append(pltpu.make_async_copy(err_in.at[rows], err_out.at[0, rows], done.at[1 + k]))
+    for copy in copies:
+        copy.start()
+    for copy in copies:
+        copy.wait()
+
+
 def per_device(inputs, out_grads, error_buf, q_prev):
     any_space = pl.BlockSpec(memory_space=pl.ANY)
 
@@ -380,7 +401,7 @@
             pltpu.VMEM((NC, NX, NY, height, width), F32),
             pltpu.VMEM((NX, NY, height, width), F32),
             stage, stage, small, small,
-            pltpu.VMEM((NZ, height, width), F32),
+            pltpu.VMEM((3, height // NZ, width), F32),
             pltpu.VMEM((NC, NX, NY, height, width), F32),
         ]
 
@@ -416,7 +437,18 @@
             collective_id=0, has_side_effects=True, vmem_limit_bytes=48 * 1024 * 1024
         ),
     )(inputs[0].T, out_grads[0], error_buf[0], q_prev)
-    return q_factor, error_next[None]
+    vmem = pl.BlockSpec(memory_space=pltpu.VMEM)
+    return pl.pallas_call(
+        closing,
+        out_shape=(
+            jax.ShapeDtypeStruct((ROWS, RANK), F32),
+            jax.ShapeDtypeStruct((1, MY_ROWS, COLS), BF16),
+        ),
+        in_specs=[vmem, vmem],
+        out_specs=(any_space, any_space),
+        scratch_shapes=[dma((5,))],
+        compiler_params=pltpu.CompilerParams(vmem_limit_bytes=1024 * 1024),
+    )(*(pltpu.with_memory_space_constraint(v, pltpu.VMEM) for v in (q_factor, error_next)))
 
 
 def solution(mesh):

time: 165 us -> 161 us (0.976)
  local copies, waits for them, and re-layouts: 4.18 us -> 0 us
    unnamed x2 -> x0, local copies, waits for them, and re-layouts: 4.18 us -> none
    pallas_call x1, Pallas kernels: 161 us -> 156 us  [per_device(): pl.pallas_call(kernel, out_shape=(pltpu.VMEM((ROWS, RANK), F32), pltpu.VM...]
    pallas_call x0 -> x1, Pallas kernels: none -> 3.54 us  [per_device(): pl.pallas_call(closing, out_shape=(jax.ShapeDtypeStruct((ROWS, RANK), F32...]
where the time goes in v3:
time: 161 us
  Pallas kernels  160 us (99%)
    pallas_call x1, Pallas kernels, per_device(): pl.pallas_call(kernel, out_shape=(pltpu.VMEM((ROWS, RANK), F32), pltpu.VM...  156 us
    pallas_call x1, Pallas kernels, per_device(): pl.pallas_call(closing, out_shape=(jax.ShapeDtypeStruct((ROWS, RANK), F32...  3.54 us

profile of v3, /device:TPU:0, one launch (start us, length us, event | category | flops | bytes accessed | tf_op | source)
XLA Modules:
  0.0 160.8 jit_solution(10225429614094007666)
XLA Ops:
  0.6 156.4 %shard_map.59 = (f32[1984,128]{1,0:T(8,128)S(1)}, bf16[496,7936]{1,0:T(8,128)(2,1)S(1)}) custom-call(bf16[1984,256]{1,0:T(8,128)(2,1)} %bitcast.7, bf16[256,7936]{1,0:T(8,128)(2,1)} %bitcast.6, bf16[496,7936]{1,0:T(8,128)(2,1)} %bitcast.5, bf16[7936,128]{1,0:T(8,128)(2,1)} %q_hbm.1), custom_call_target="tpu_custom_call" | custom-call | tf_op jit(solution)/shard_map/pallas_call | solution.py:409
  157.1 3.5 %shard_map.60 = (f32[1984,128]{1,0:T(8,128)}, bf16[1,496,7936]{2,1,0:T(8,128)(2,1)}) custom-call(f32[1984,128]{1,0:T(8,128)S(1)} %get-tuple-element.4.qf_in, bf16[496,7936]{1,0:T(8,128)(2,1)S(1)} %get-tuple-element.5.err_in), custom_call_target="tpu_custom_call" | custom-call | tf_op jit(solution)/shard_map/pallas_call | solution.py:441

commit v4 on v3

--- a/solution.py
+++ b/solution.py
@@ -19,6 +19,7 @@
 P_SLICE = P_ROWS // 32
 PIECES = ((0, 5), (5, 10), (10, 15), (15, 20), (20, 24), (24, 28), (28, 30), (30, 31))
 N_PIECE = len(PIECES)
+TAIL = 28
 N_COPY = 32
 PANEL = 32
 PLAN = {
@@ -39,6 +40,16 @@
 def split(value):
     high = value.astype(BF16)
     return high, (value - high.astype(F32)).astype(BF16)
+
+
+def stacked(q_block):
+    high, low = split(q_block)
+    return jnp.concatenate([high, high, low], axis=0)
+
+
+def error_block(xr, g_all, e_buf, p_cat, cols, q_cat):
+    merged = dot(xr[...], g_all[:, cols]) + e_buf[:, cols].astype(F32)
+    return (merged - dot(p_cat[...], q_cat)).astype(BF16)
 
 
 def all_reduce(part, from_core, r1x, r1y, r2x, r2y, rz, full, send, recv, place, scale):
@@ -180,8 +191,8 @@
 
 
 def kernel(
-    xt_hbm, g_hbm, e_hbm, q_hbm, qf_out, e_buf,
-    xt, xr, g_all, q_in, p_flat, t_cat, mat, p_rows, p_t, y_cat, p_cat, q_lines,
+    xt_hbm, g_hbm, e_hbm, q_hbm, qf_out, e_buf, xr, g_all, p_cat, q_tail,
+    xt, q_in, p_flat, t_cat, mat, p_rows, p_t, y_cat, q_lines,
     p_part, p_core, p1x, p1y, p2x, p2y, p_z, p_full,
     q_part, q_core, q1x, q1y, q2x, q2y, q_z, q_full,
     load, store, p_send, p_recv, q_send, q_recv, x_send, x_recv, g_send, g_recv,
@@ -350,6 +361,8 @@
         qf_store = pltpu.make_async_copy(q_lines.at[pl.ds(offset, ROWS)], qf_out, store.at[0])
         qf_store.start()
 
+    for s in range(TAIL, CHUNKS):
+        q_tail[s - TAIL] = stacked(q_full[s // 16, (s // 4) % 4, s % 4])
     loads[4].wait()
     for copy in x_copies:
         copy.wait_recv()
@@ -362,14 +375,13 @@
 
         def error_chunk(s, carry):
             cols = pl.ds(pl.multiple_of(s * CHUNK, CHUNK), CHUNK)
-            q_high, q_low = split(q_full[s // 16, (s // 4) % 4, s % 4])
-            merged = dot(xr[...], g_all[:, cols]) + e_buf[:, cols].astype(F32)
-            update = dot(p_cat[...], jnp.concatenate([q_high, q_high, q_low], axis=0))
-            e_buf[:, cols] = (merged - update).astype(BF16)
+            q_cat = stacked(q_full[s // 16, (s // 4) % 4, s % 4])
+            e_buf[:, cols] = error_block(xr, g_all, e_buf, p_cat, cols, q_cat)
             return carry
 
-        with jax.named_scope("error_next"):
-            lax.fori_loop(first, last, error_chunk, 0)
+        if last <= TAIL:
+            with jax.named_scope("error_next"):
+                lax.fori_loop(first, last, error_chunk, 0)
 
     with jax.named_scope("finish"):
         p_sent()
@@ -380,19 +392,25 @@
             copy.wait()
 
 
-def closing(qf_in, err_in, qf_out, err_out, done):
+def closing(qf_in, e_buf, xr, g_all, p_cat, q_tail, qf_out, err_out, tail, done):
     copies = [pltpu.make_async_copy(qf_in, qf_out, done.at[0])]
-    for k, (first, last) in enumerate(((0, 128), (128, 256), (256, 384), (384, MY_ROWS))):
-        rows = pl.ds(first, last - first)
-        copies.append(pltpu.make_async_copy(err_in.at[rows], err_out.at[0, rows], done.at[1 + k]))
+    for k in range(4):
+        cols = pl.ds(k * TAIL // 4 * CHUNK, TAIL // 4 * CHUNK)
+        copies.append(pltpu.make_async_copy(e_buf.at[:, cols], err_out.at[0, :, cols], done.at[1 + k]))
     for copy in copies:
         copy.start()
+    for i in range(CHUNKS - TAIL):
+        cols = pl.ds((TAIL + i) * CHUNK, CHUNK)
+        tail[i] = error_block(xr, g_all, e_buf, p_cat, cols, q_tail[i])
+        copies.append(pltpu.make_async_copy(tail.at[i], err_out.at[0, :, cols], done.at[5 + i]))
+        copies[-1].start()
     for copy in copies:
         copy.wait()
 
 
 def per_device(inputs, out_grads, error_buf, q_prev):
     any_space = pl.BlockSpec(memory_space=pl.ANY)
+    vmem = pl.BlockSpec(memory_space=pltpu.VMEM)
 
     def reduce_scratch(height, width):
         stage = pltpu.VMEM((3, 4, height // 2, width), F32)
@@ -406,18 +424,20 @@
         ]
 
     dma = pltpu.SemaphoreType.DMA
-    q_factor, error_next = pl.pallas_call(
+    held = pl.pallas_call(
         kernel,
         out_shape=(
             pltpu.VMEM((ROWS, RANK), F32),
             pltpu.VMEM((MY_ROWS, COLS), BF16),
+            pltpu.VMEM((MY_ROWS, NZ * TOKENS), BF16),
+            pltpu.VMEM((NZ * TOKENS, COLS), BF16),
+            pltpu.VMEM((MY_ROWS, 3 * RANK), BF16),
+            pltpu.VMEM((CHUNKS - TAIL, 3 * RANK, CHUNK), BF16),
         ),
         in_specs=[any_space] * 4,
-        out_specs=(pl.BlockSpec(memory_space=pltpu.VMEM),) * 2,
+        out_specs=(vmem,) * 6,
         scratch_shapes=[
             pltpu.VMEM((P_ROWS, TOKENS), BF16),
-            pltpu.VMEM((MY_ROWS, NZ * TOKENS), BF16),
-            pltpu.VMEM((NZ * TOKENS, COLS), BF16),
             pltpu.VMEM((COLS, RANK), BF16),
             pltpu.VMEM((P_ROWS, RANK), F32),
             pltpu.VMEM((TOKENS, 2 * RANK), BF16),
@@ -425,7 +445,6 @@
             pltpu.VMEM((2 * RANK, P_ROWS), BF16),
             pltpu.VMEM((2 * RANK, MY_ROWS), BF16),
             pltpu.VMEM((2 * RANK, TOKENS), BF16),
-            pltpu.VMEM((MY_ROWS, 3 * RANK), BF16),
             pltpu.VMEM((9 * CHUNK, RANK), F32),
             *reduce_scratch(P_SLICE, RANK),
             *reduce_scratch(RANK, CHUNK),
@@ -434,21 +453,23 @@
             dma((4,)), dma((4,)), dma((6, N_PIECE)), dma((6, N_PIECE)),
         ],
         compiler_params=pltpu.CompilerParams(
-            collective_id=0, has_side_effects=True, vmem_limit_bytes=48 * 1024 * 1024
+            collective_id=0, has_side_effects=True, vmem_limit_bytes=32 * 1024 * 1024
         ),
     )(inputs[0].T, out_grads[0], error_buf[0], q_prev)
-    vmem = pl.BlockSpec(memory_space=pltpu.VMEM)
     return pl.pallas_call(
         closing,
         out_shape=(
             jax.ShapeDtypeStruct((ROWS, RANK), F32),
             jax.ShapeDtypeStruct((1, MY_ROWS, COLS), BF16),
         ),
-        in_specs=[vmem, vmem],
+        in_specs=[vmem] * 6,
         out_specs=(any_space, any_space),
-        scratch_shapes=[dma((5,))],
-        compiler_params=pltpu.CompilerParams(vmem_limit_bytes=1024 * 1024),
-    )(*(pltpu.with_memory_space_constraint(v, pltpu.VMEM) for v in (q_factor, error_next)))
+        scratch_shapes=[
+            pltpu.VMEM((CHUNKS - TAIL, MY_ROWS, CHUNK), BF16),
+            dma((5 + CHUNKS - TAIL,)),
+        ],
+        compiler_params=pltpu.CompilerParams(vmem_limit_bytes=6 * 1024 * 1024),
+    )(*(pltpu.with_memory_space_constraint(v, pltpu.VMEM) for v in held))
 
 
 def solution(mesh):

time: 161 us -> 160 us (level)
  no operation moved by 1% of the time
where the time goes in v4:
time: 160 us
  Pallas kernels  159 us (99%)
    pallas_call x1, Pallas kernels, per_device(): pl.pallas_call(kernel, out_shape=(pltpu.VMEM((ROWS, RANK), F32), pltpu.VM...  155 us
    pallas_call x1, Pallas kernels, per_device(): pl.pallas_call(closing, out_shape=(jax.ShapeDtypeStruct((ROWS, RANK), F32...  3.5 us

profile of v4, /device:TPU:0, one launch (start us, length us, event | category | flops | bytes accessed | tf_op | source)
XLA Modules:
  0.0 159.7 jit_solution(10558328527371216548)
XLA Ops:
  0.6 155.4 %shard_map.59 = (f32[1984,128]{1,0:T(8,128)S(1)}, bf16[496,7936]{1,0:T(8,128)(2,1)S(1)}, bf16[496,1024]{1,0:T(8,128)(2,1)S(1)}, bf16[1024,7936]{1,0:T(8,128)(2,1...) custom-call(bf16[1984,256]{1,0:T(8,128)(2,1)} %bitcast.7, bf16[256,7936]{1,0:T(8,128)(2,1)} %bitcast.6, ...), custom_call_target="tpu_custom_call" | custom-call | tf_op jit(solution)/shard_map/pallas_call | solution.py:427
  156.0 3.5 %shard_map.60 = (f32[1984,128]{1,0:T(8,128)}, bf16[1,496,7936]{2,1,0:T(8,128)(2,1)}) custom-call(f32[1984,128]{1,0:T(8,128)S(1)} %get-tuple-element.8.qf_in, bf16[496,7936]{1,0:T(8,128)(2,1)S(1)} %get-tuple-element.9.e_buf, bf16[496,1024]{1,0:T(8,128)(2,1)S(1)} %get-tuple-element.10.xr, bf16[1024,7936]{1,0:T(8,128)(2,1)S(1)} %get-tuple-element.11.g_all, ...), custom_call_target="tpu_custom_call" | custom-call | tf_op jit(solution)/shard_map/pallas_call | solution.py:459

commit v5 on v4

--- a/solution.py
+++ b/solution.py
@@ -20,14 +20,16 @@
 PIECES = ((0, 5), (5, 10), (10, 15), (15, 20), (20, 24), (24, 28), (28, 30), (30, 31))
 N_PIECE = len(PIECES)
 TAIL = 28
-N_COPY = 32
+N_COPY = 34
 PANEL = 32
 PLAN = {
     "start": (("x", 0, 3), ("early", 0, 2)),
     "p4": (("early", 6, 8),),
     "p5": (("early", 2, 6), ("late", 0, 4)),
-    "q4": (("late", 6, 8),),
-    "q5": (("late", 4, 6), ("onward", 0, 8)),
+    "q4": (("late", 6, 7),),
+    "q5": (("late", 4, 5),),
+    "q6": (("late", 5, 6),),
+    "q7": (("late", 7, 8), ("onward", 0, 8)),
 }
 
 
@@ -42,6 +44,10 @@
     return high, (value - high.astype(F32)).astype(BF16)
 
 
+def slot(s):
+    return s % NC, s // (NC * NY), s // NC % NY
+
+
 def stacked(q_block):
     high, low = split(q_block)
     return jnp.concatenate([high, high, low], axis=0)
@@ -52,14 +58,20 @@
     return (merged - dot(p_cat[...], q_cat)).astype(BF16)
 
 
-def all_reduce(part, from_core, r1x, r1y, r2x, r2y, rz, full, send, recv, place, scale):
+def all_reduce(part, from_core, r1x, r1y, r2x, r2y, rz_half, rz, full, send, recv, place, scale, relayed):
     x, y, core, z = place
     height = part.shape[3]
     upper, lower = pl.ds(0, height // 2), pl.ds(height // 2, height // 2)
     running = {}
 
+    up, across_z, down = (z + 1) % NZ, (z + 2) % NZ, (z + 3) % NZ
+
     def quarter(k):
         return pl.ds(pl.multiple_of(k * (height // NZ), 8), height // NZ)
+
+    def half(k, which):
+        size = height // NZ // 2
+        return pl.ds(pl.multiple_of(k * 2 * size + which * size, 8), size)
 
     def start(key, number, src, dst, where):
         px, py, pcore, pz = where
@@ -108,20 +120,45 @@
         arrive("2y")
         part[core, x, y, upper] = part[core, x, y, upper] + r2y[0] + r2y[1] + r2y[2]
         part[core, x, y, lower] = part[core, x, y, lower] + r2x[0] + r2x[1] + r2x[2]
-        for d in range(1, 4):
-            to = (z + d) % NZ
-            start("z", 12 + d, part.at[core, x, y, quarter(to)], rz.at[d - 1], (x, y, core, to))
+        mine = part.at[core, x, y]
+        if not relayed:
+            for d in range(1, 4):
+                to = (z + d) % NZ
+                start("zb", 12 + d, mine.at[quarter(to)], rz.at[d - 1], (x, y, core, to))
+            return
+        start("za", 13, mine.at[half(across_z, 0)], rz_half.at[0], (x, y, core, up))
+        start("za", 14, mine.at[half(across_z, 1)], rz_half.at[1], (x, y, core, down))
+
+    def relay():
+        arrive("za")
+        part[core, x, y, half(up, 0)] = part[core, x, y, half(up, 0)] + rz_half[0]
+        part[core, x, y, half(down, 1)] = part[core, x, y, half(down, 1)] + rz_half[1]
+        mine = part.at[core, x, y]
+        start("zb", 15, mine.at[quarter(up)], rz.at[0], (x, y, core, up))
+        start("zb", 29, mine.at[quarter(down)], rz.at[1], (x, y, core, down))
 
     def total():
-        arrive("z")
+        arrive("zb")
         mine = quarter(z)
-        full[core, x, y, mine] = (part[core, x, y, mine] + rz[0] + rz[1] + rz[2]) * scale
-        for d in range(1, 4):
-            mine = full.at[core, x, y, quarter(z)]
-            start("zz", 28 + d, mine, mine, (x, y, core, (z + d) % NZ))
+        others = rz[0] + rz[1] if relayed else rz[0] + rz[1] + rz[2]
+        full[core, x, y, mine] = (part[core, x, y, mine] + others) * scale
+        mine = full.at[core, x, y, quarter(z)]
+        if not relayed:
+            for d in range(1, 4):
+                start("zd", 28 + d, mine, mine, (x, y, core, (z + d) % NZ))
+            return
+        start("zc", 30, mine, mine, (x, y, core, up))
+        start("zc", 31, mine, mine, (x, y, core, down))
+
+    def onward():
+        arrive("zc")
+        mine = full.at[core, x, y, half(down, 0)]
+        start("zd", 32, mine, mine, (x, y, core, up))
+        mine = full.at[core, x, y, half(up, 1)]
+        start("zd", 33, mine, mine, (x, y, core, down))
 
     def joined():
-        arrive("zz")
+        arrive("zd")
         for d in range(1, 4):
             px, py = (x + d) % NX, (y + d) % NY
             mine = full.at[core, x, y, upper]
@@ -152,6 +189,8 @@
             for copy in copies:
                 copy.wait_send()
 
+    if relayed:
+        return [begin, first, second, across, relay, total, onward, joined, spread, share, end], sent
     return [begin, first, second, across, total, joined, spread, share, end], sent
 
 
@@ -193,14 +232,29 @@
 def kernel(
     xt_hbm, g_hbm, e_hbm, q_hbm, qf_out, e_buf, xr, g_all, p_cat, q_tail,
     xt, q_in, p_flat, t_cat, mat, p_rows, p_t, y_cat, q_lines,
-    p_part, p_core, p1x, p1y, p2x, p2y, p_z, p_full,
-    q_part, q_core, q1x, q1y, q2x, q2y, q_z, q_full,
+    p_part, p_core, p1x, p1y, p2x, p2y, p_zh, p_z, p_full,
+    q_part, q_core, q1x, q1y, q2x, q2y, q_zh, q_z, q_full,
     load, store, p_send, p_recv, q_send, q_recv, x_send, x_recv, g_send, g_recv,
 ):
     m, z = lax.axis_index("machine"), lax.axis_index("local")
     core, y, x = m % NC, (m // NC) % NY, m // (NC * NY)
     place = (x, y, core, z)
     left, right = (z + NZ - 1) % NZ, (z + 1) % NZ
+
+    with jax.named_scope("barrier"):
+        barrier = pltpu.get_barrier_semaphore()
+        for d in range(1, 4):
+            for px, py, pcore, pz in (
+                (x, y, core, (z + d) % NZ), ((x + d) % NX, y, core, z), (x, (y + d) % NY, core, z)
+            ):
+                pl.semaphore_signal(
+                    barrier, inc=1, device_id_type=MESH,
+                    device_id={"machine": (px * NY + py) * NC + pcore, "local": pz},
+                )
+        pl.semaphore_signal(
+            barrier, inc=1, device_id_type=MESH,
+            device_id={"machine": (x * NY + y) * NC + 1 - core, "local": z},
+        )
 
     loads = [
         pltpu.make_async_copy(g_hbm, g_all.at[pl.ds(z * TOKENS, TOKENS)], load.at[0]),
@@ -214,21 +268,7 @@
     for copy in loads:
         copy.start()
 
-    with jax.named_scope("barrier"):
-        barrier = pltpu.get_barrier_semaphore()
-        for d in range(1, 4):
-            for px, py, pcore, pz in (
-                ((x + d) % NX, y, core, z), (x, (y + d) % NY, core, z), (x, y, core, (z + d) % NZ)
-            ):
-                pl.semaphore_signal(
-                    barrier, inc=1, device_id_type=MESH,
-                    device_id={"machine": (px * NY + py) * NC + pcore, "local": pz},
-                )
-        pl.semaphore_signal(
-            barrier, inc=1, device_id_type=MESH,
-            device_id={"machine": (x * NY + y) * NC + 1 - core, "local": z},
-        )
-        pl.semaphore_wait(barrier, 10)
+    pl.semaphore_wait(barrier, 10)
 
     x_copies = []
     for d in range(1, 4):
@@ -273,10 +313,10 @@
     due("start")
 
     p_steps, p_sent = all_reduce(
-        p_part, p_core, p1x, p1y, p2x, p2y, p_z, p_full, p_send, p_recv, place, 1.0 / 32
+        p_part, p_core, p1x, p1y, p2x, p2y, p_zh, p_z, p_full, p_send, p_recv, place, 1.0 / 32, False
     )
     q_steps, q_sent = all_reduce(
-        q_part, q_core, q1x, q1y, q2x, q2y, q_z, q_full, q_send, q_recv, place, 1.0 / 32
+        q_part, q_core, q1x, q1y, q2x, q2y, q_zh, q_z, q_full, q_send, q_recv, place, 1.0 / 32, True
     )
 
     with jax.named_scope("left_terms"):
@@ -330,66 +370,76 @@
 
         q_part[1, 3, 3] = jnp.zeros((RANK, CHUNK), F32)
 
-        def right_terms(s, carry):
-            cols = pl.ds(pl.multiple_of(s * CHUNK, CHUNK), CHUNK)
-            both = dot(y_cat[...], g_all[own, cols]) + dot(p_t[...], e_buf[:, cols])
-            q_part[s // 16, (s // 4) % 4, s % 4] = both[0:RANK] + both[RANK : 2 * RANK]
-            return carry
-
-        other = (1 - core) * 16
-        lax.fori_loop(other, other + 15 + core, right_terms, 0)
+        def right_terms(which):
+            def chunk(i, carry):
+                s = NC * i + which
+                cols = pl.ds(pl.multiple_of(s * CHUNK, CHUNK), CHUNK)
+                both = dot(y_cat[...], g_all[own, cols]) + dot(p_t[...], e_buf[:, cols])
+                q_part[slot(s)] = both[0:RANK] + both[RANK : 2 * RANK]
+                return carry
+
+            lax.fori_loop(0, 16 - which, chunk, 0)
+
+        right_terms(1 - core)
         due("q0")
         q_steps[0]()
-        lax.fori_loop(core * 16, core * 16 + 16 - core, right_terms, 0)
-
-    for k, step in enumerate(q_steps[1:], 1):
+        right_terms(core)
+
+    for k, step in enumerate(q_steps[1:-1], 1):
         due("q%d" % k)
         step()
 
+    loads[4].wait()
+    for copy in x_copies:
+        copy.wait_recv()
+
+    def wait_piece(i):
+        for copy in late[2 * i : 2 * i + 2] + onward[2 * i : 2 * i + 2]:
+            copy.wait_recv()
+
+    def error_chunk(s, carry):
+        cols = pl.ds(pl.multiple_of(s * CHUNK, CHUNK), CHUNK)
+        e_buf[:, cols] = error_block(xr, g_all, e_buf, p_cat, cols, stacked(q_full[slot(s)]))
+        return carry
+
+    with jax.named_scope("error_next"):
+        wait_piece(0)
+        wait_piece(1)
+        ahead = PIECES[1][1] // NC
+        lax.fori_loop(0, ahead, lambda i, carry: error_chunk(NC * i + core, carry), 0)
+        q_steps[-1]()
+        lax.fori_loop(0, ahead, lambda i, carry: error_chunk(NC * i + 1 - core, carry), 0)
+        for i in range(2, N_PIECE - 3):
+            wait_piece(i)
+            lax.fori_loop(*PIECES[i], error_chunk, 0)
+
     with jax.named_scope("right_factor"):
         first_line = (31 * z) // 4
 
         def lines(i, carry):
             s = first_line + i
-            q_lines[pl.ds(pl.multiple_of(i * CHUNK, CHUNK), CHUNK), :] = q_full[
-                s // 16, (s // 4) % 4, s % 4
-            ].T
+            q_lines[pl.ds(pl.multiple_of(i * CHUNK, CHUNK), CHUNK), :] = q_full[slot(s)].T
             return carry
 
         lax.fori_loop(0, 9, lines, 0)
         offset = (CHUNK - 64 * z) % CHUNK
         qf_store = pltpu.make_async_copy(q_lines.at[pl.ds(offset, ROWS)], qf_out, store.at[0])
         qf_store.start()
-
-    for s in range(TAIL, CHUNKS):
-        q_tail[s - TAIL] = stacked(q_full[s // 16, (s // 4) % 4, s % 4])
-    loads[4].wait()
-    for copy in x_copies:
-        copy.wait_recv()
-    stores = [qf_store]
-    for i in range(N_PIECE):
-        first, last = PIECES[i]
-        with jax.named_scope("error_wait"):
-            for copy in late[2 * i : 2 * i + 2] + onward[2 * i : 2 * i + 2]:
-                copy.wait_recv()
-
-        def error_chunk(s, carry):
-            cols = pl.ds(pl.multiple_of(s * CHUNK, CHUNK), CHUNK)
-            q_cat = stacked(q_full[s // 16, (s // 4) % 4, s % 4])
-            e_buf[:, cols] = error_block(xr, g_all, e_buf, p_cat, cols, q_cat)
-            return carry
-
-        if last <= TAIL:
-            with jax.named_scope("error_next"):
-                lax.fori_loop(first, last, error_chunk, 0)
+        for s in range(TAIL, CHUNKS):
+            q_tail[s - TAIL] = stacked(q_full[slot(s)])
+
+    with jax.named_scope("error_next_end"):
+        wait_piece(N_PIECE - 3)
+        lax.fori_loop(*PIECES[N_PIECE - 3], error_chunk, 0)
+        wait_piece(N_PIECE - 2)
+        wait_piece(N_PIECE - 1)
 
     with jax.named_scope("finish"):
         p_sent()
         q_sent()
         for copy in x_copies + early + late + onward:
             copy.wait_send()
-        for copy in stores:
-            copy.wait()
+        qf_store.wait()
 
 
 def closing(qf_in, e_buf, xr, g_all, p_cat, q_tail, qf_out, err_out, tail, done):
@@ -419,6 +469,7 @@
             pltpu.VMEM((NC, NX, NY, height, width), F32),
             pltpu.VMEM((NX, NY, height, width), F32),
             stage, stage, small, small,
+            pltpu.VMEM((2, height // NZ // 2, width), F32),
             pltpu.VMEM((3, height // NZ, width), F32),
             pltpu.VMEM((NC, NX, NY, height, width), F32),
         ]

time: 160 us -> 159 us (level)
  no operation moved by 1% of the time
where the time goes in v5:
time: 159 us
  Pallas kernels  158 us (99%)
    pallas_call x1, Pallas kernels, per_device(): pl.pallas_call(kernel, out_shape=(pltpu.VMEM((ROWS, RANK), F32), pltpu.VM...  155 us
    pallas_call x1, Pallas kernels, per_device(): pl.pallas_call(closing, out_shape=(jax.ShapeDtypeStruct((ROWS, RANK), F32...  3.5 us

profile of v5, /device:TPU:0, one launch (start us, length us, event | category | flops | bytes accessed | tf_op | source)
XLA Modules:
  0.0 159.1 jit_solution(2986264957062278144)
XLA Ops:
  0.6 154.8 %shard_map.59 = (f32[1984,128]{1,0:T(8,128)S(1)}, bf16[496,7936]{1,0:T(8,128)(2,1)S(1)}, bf16[496,1024]{1,0:T(8,128)(2,1)S(1)}, bf16[1024,7936]{1,0:T(8,128)(2,1...) custom-call(bf16[1984,256]{1,0:T(8,128)(2,1)} %bitcast.7, bf16[256,7936]{1,0:T(8,128)(2,1)} %bitcast.6, ...), custom_call_target="tpu_custom_call" | custom-call | tf_op jit(solution)/shard_map/pallas_call | solution.py:478
  155.4 3.5 %shard_map.60 = (f32[1984,128]{1,0:T(8,128)}, bf16[1,496,7936]{2,1,0:T(8,128)(2,1)}) custom-call(f32[1984,128]{1,0:T(8,128)S(1)} %get-tuple-element.8.qf_in, bf16[496,7936]{1,0:T(8,128)(2,1)S(1)} %get-tuple-element.9.e_buf, bf16[496,1024]{1,0:T(8,128)(2,1)S(1)} %get-tuple-element.10.xr, bf16[1024,7936]{1,0:T(8,128)(2,1)S(1)} %get-tuple-element.11.g_all, ...), custom_call_target="tpu_custom_call" | custom-call | tf_op jit(solution)/shard_map/pallas_call | solution.py:510

commit v6 on v5

--- a/solution.py
+++ b/solution.py
@@ -431,15 +431,17 @@
     with jax.named_scope("error_next_end"):
         wait_piece(N_PIECE - 3)
         lax.fori_loop(*PIECES[N_PIECE - 3], error_chunk, 0)
+        p_sent()
+        q_sent()
+        for copy in x_copies + early + late + onward[:-4]:
+            copy.wait_send()
+        qf_store.wait()
+
+    with jax.named_scope("finish"):
         wait_piece(N_PIECE - 2)
         wait_piece(N_PIECE - 1)
-
-    with jax.named_scope("finish"):
-        p_sent()
-        q_sent()
-        for copy in x_copies + early + late + onward:
+        for copy in onward[-4:]:
             copy.wait_send()
-        qf_store.wait()
 
 
 def closing(qf_in, e_buf, xr, g_all, p_cat, q_tail, qf_out, err_out, tail, done):

time: 159 us -> 159 us (level)
  no operation moved by 1% of the time
where the time goes in v6:
time: 159 us
  Pallas kernels  158 us (99%)
    pallas_call x1, Pallas kernels, per_device(): pl.pallas_call(kernel, out_shape=(pltpu.VMEM((ROWS, RANK), F32), pltpu.VM...  155 us
    pallas_call x1, Pallas kernels, per_device(): pl.pallas_call(closing, out_shape=(jax.ShapeDtypeStruct((ROWS, RANK), F32...  3.5 us

profile of v6, /device:TPU:0, one launch (start us, length us, event | category | flops | bytes accessed | tf_op | source)
XLA Modules:
  0.0 158.9 jit_solution(10706690590639601912)
XLA Ops:
  0.6 154.6 %shard_map.59 = (f32[1984,128]{1,0:T(8,128)S(1)}, bf16[496,7936]{1,0:T(8,128)(2,1)S(1)}, bf16[496,1024]{1,0:T(8,128)(2,1)S(1)}, bf16[1024,7936]{1,0:T(8,128)(2,1...) custom-call(bf16[1984,256]{1,0:T(8,128)(2,1)} %bitcast.7, bf16[256,7936]{1,0:T(8,128)(2,1)} %bitcast.6, ...), custom_call_target="tpu_custom_call" | custom-call | tf_op jit(solution)/shard_map/pallas_call | solution.py:480
  155.2 3.5 %shard_map.60 = (f32[1984,128]{1,0:T(8,128)}, bf16[1,496,7936]{2,1,0:T(8,128)(2,1)}) custom-call(f32[1984,128]{1,0:T(8,128)S(1)} %get-tuple-element.8.qf_in, bf16[496,7936]{1,0:T(8,128)(2,1)S(1)} %get-tuple-element.9.e_buf, bf16[496,1024]{1,0:T(8,128)(2,1)S(1)} %get-tuple-element.10.xr, bf16[1024,7936]{1,0:T(8,128)(2,1)S(1)} %get-tuple-element.11.g_all, ...), custom_call_target="tpu_custom_call" | custom-call | tf_op jit(solution)/shard_map/pallas_call | solution.py:512

commit v7 on v6

--- a/solution.py
+++ b/solution.py
@@ -23,13 +23,13 @@
 N_COPY = 34
 PANEL = 32
 PLAN = {
-    "start": (("x", 0, 3), ("early", 0, 2)),
-    "p4": (("early", 6, 8),),
-    "p5": (("early", 2, 6), ("late", 0, 4)),
-    "q4": (("late", 6, 7),),
-    "q5": (("late", 4, 5),),
-    "q6": (("late", 5, 6),),
-    "q7": (("late", 7, 8), ("onward", 0, 8)),
+    "start": (("early", 0, 2), ("x", 0, 3)),
+    "p4": (("early", 2, 3),),
+    "p5": (("early", 3, 8), ("late", 0, 4)),
+    "q4": (("late", 4, 5),),
+    "q5": (("late", 5, 6),),
+    "q6": (("late", 6, 8),),
+    "q7": (("onward", 0, 8),),
 }
 
 

time: 159 us -> 159 us (level)
  no operation moved by 1% of the time
where the time goes in v7:
time: 159 us
  Pallas kernels  158 us (99%)
    pallas_call x1, Pallas kernels, per_device(): pl.pallas_call(kernel, out_shape=(pltpu.VMEM((ROWS, RANK), F32), pltpu.VM...  155 us
    pallas_call x1, Pallas kernels, per_device(): pl.pallas_call(closing, out_shape=(jax.ShapeDtypeStruct((ROWS, RANK), F32...  3.5 us

profile of v7, /device:TPU:0, one launch (start us, length us, event | category | flops | bytes accessed | tf_op | source)
XLA Modules:
  0.0 158.9 jit_solution(3262157462884698704)
XLA Ops:
  0.6 154.6 %shard_map.59 = (f32[1984,128]{1,0:T(8,128)S(1)}, bf16[496,7936]{1,0:T(8,128)(2,1)S(1)}, bf16[496,1024]{1,0:T(8,128)(2,1)S(1)}, bf16[1024,7936]{1,0:T(8,128)(2,1...) custom-call(bf16[1984,256]{1,0:T(8,128)(2,1)} %bitcast.7, bf16[256,7936]{1,0:T(8,128)(2,1)} %bitcast.6, ...), custom_call_target="tpu_custom_call" | custom-call | tf_op jit(solution)/shard_map/pallas_call | solution.py:480
  155.2 3.5 %shard_map.60 = (f32[1984,128]{1,0:T(8,128)}, bf16[1,496,7936]{2,1,0:T(8,128)(2,1)}) custom-call(f32[1984,128]{1,0:T(8,128)S(1)} %get-tuple-element.8.qf_in, bf16[496,7936]{1,0:T(8,128)(2,1)S(1)} %get-tuple-element.9.e_buf, bf16[496,1024]{1,0:T(8,128)(2,1)S(1)} %get-tuple-element.10.xr, bf16[1024,7936]{1,0:T(8,128)(2,1)S(1)} %get-tuple-element.11.g_all, ...), custom_call_target="tpu_custom_call" | custom-call | tf_op jit(solution)/shard_map/pallas_call | solution.py:512
